TPU v7x, 256 devices: a whole 4x4x8 slice. The times are simulated.
256 devices in a mesh: row: 4 (over y), col: 64 (over x, z, core).
Axes of the slice: x: 4, y: 4, z: 8, core: 2. Of those that a mesh axis runs over, the one named last changes fastest.
Arguments:
- slide_band: bfloat16 [3, 64, 32768], P(None, 'row', 'col'), may hold values from -21 to 21
- cotangent: bfloat16 [64, 32, 16384], P(None, 'row', 'col'), may hold values from -0.058004853 to 0.058004853
- stem_weight: bfloat16 [64, 7, 7, 3], replicated, may hold values from -0.5 to 0.5
- mid_weight: bfloat16 [2, 64, 3, 3, 64], replicated, may hold values from -0.25 to 0.25
- norm_gains: float32 [3, 64], replicated, may hold values from 0.1 to 1.9
- norm_shifts: float32 [3, 64], replicated, may hold values from -0.5 to 0.5
Outputs:
- activation: bfloat16 [64, 32, 16384], P(None, 'row', 'col')
- grad_stem: float32 [64, 7, 7, 3], replicated
- grad_mid: float32 [2, 64, 3, 3, 64], replicated
- grad_gains: float32 [3, 64], replicated
- grad_shifts: float32 [3, 64], replicated
All inputs are finite; a program needn't handle non-finite values.
Results may differ from a plain program's by a relative error of at most 0.005.
The roundings to bfloat16 on the way count: a program that leaves them out, or rounds other values in their place, can miss the bound.
Values may be sent and summed in bfloat16 or wider, within the bound.
A program may use at most 64 MiB of HBM per device.

v0:
```python
import jax
import jax.numpy as jnp
from jax import lax
from jax.experimental import pallas as pl
from jax.experimental.pallas import tpu as pltpu
from jax.sharding import PartitionSpec as P

EPS = 1e-05
MESH = pl.DeviceIdType.MESH
F32 = jnp.float32
BF16 = jnp.bfloat16

CH = 64
ROWS = 8
COLS = 256
TAPS = 9 * CH
LOCAL = ROWS * COLS
PIXELS = 524288.0
CHIPS = 128
VMEM_BYTES = 62 * 1024 * 1024
PLANE = 32
DEPTH = 8
STEM_ROWS = 21


def dot(a, b):
    return jnp.dot(a, b, preferred_element_type=F32)


def dot_nt(a, b):
    return lax.dot_general(a, b, (((1,), (1,)), ((), ())), preferred_element_type=F32)


def hops(offset):
    return sum(min(d, n - d) for d, n in zip(offset, (4, 4, 8)))


CHIP_OFFSETS = sorted(
    ((dy, dx, dz) for dy in range(4) for dx in range(4) for dz in range(8) if dy or dx or dz),
    key=lambda offset: -hops(offset),
)
PLANE_OFFSETS = sorted(
    ((dy, dx, dc) for dy in range(4) for dx in range(4) for dc in range(2) if dy or dx or dc),
    key=lambda offset: -hops((offset[0], offset[1], 0)),
)
DEPTH_OFFSETS = (4, 3, 5, 2, 6, 1, 7)


def kernel(
    img, cot, w0_in, wm_in, gains_in, shifts_in,
    act_hbm, stem_hbm, mid_hbm, gains_hbm, shifts_hbm,
    act_out, stem_out, mid_out, gains_out, shifts_out,
    cot_raw, w0_raw, wm_raw, norm_raw, w0_flat, wm, wt, cot_flat, cot_rows, act_rows, choose,
    tiles, sel, patches, wbig, x0, x1, dmap, dstem,
    pre, white, slope, up, rowhalo, colsend, colrecv,
    first_a, first_b, ar_a, ar_b, gsend, grecv, gdepth, gfull, ssend, srecv, sdepth, sfull, rows_full,
    in_sem, out_sem, img_send, img_recv, halo_send, halo_recv, ar_send, ar_recv, fin_send, fin_recv,
):
    row, col = lax.axis_index("row"), lax.axis_index("col")
    chip_x, chip_z, core = lax.div(col, 16), lax.rem(lax.div(col, 2), 8), lax.rem(col, 2)
    not_top = jnp.where(row == 0, 0.0, 1.0).astype(F32)
    not_bottom = jnp.where(row == 3, 0.0, 1.0).astype(F32)
    not_left = jnp.where(col == 0, 0.0, 1.0).astype(F32)
    not_right = jnp.where(col == 63, 0.0, 1.0).astype(F32)
    chip_rank = (row * 4 + chip_x) * 8 + chip_z
    plane_rank = (row * 4 + chip_x) * 2 + core

    ring_y = [row] + [lax.rem(row + d, 4) for d in range(1, 4)]
    ring_x = [chip_x] + [lax.rem(chip_x + d, 4) for d in range(1, 4)]
    ring_z = [2 * chip_z + core] + [2 * lax.rem(chip_z + d, 8) + core for d in range(1, 8)]
    ring_core = [core, 1 - core]
    col_x = [16 * x for x in ring_x]
    col_core = [2 * chip_z + c for c in ring_core]
    other_core = (row, col_x[0] + col_core[1])

    def chip_peer(offset):
        dy, dx, dz = offset
        return (ring_y[dy], col_x[dx] + ring_z[dz])

    def plane_peer(offset):
        dy, dx, dc = offset
        return 8 * ring_y[dy] + 2 * ring_x[dx] + ring_core[dc], (ring_y[dy], col_x[dx] + col_core[dc])

    def depth_peer(dz):
        return (row, col_x[0] + ring_z[dz])

    def near(dr, dc):
        return (lax.rem(row + dr + 4, 4), lax.rem(col + dc + 64, 64))

    around = [(1, 0), (-1, 0), (0, 1), (0, -1), (1, 1), (1, -1), (-1, 1), (-1, -1)]

    barrier = pltpu.get_barrier_semaphore()

    def greet(where):
        pl.semaphore_signal(barrier, inc=1, device_id=where, device_id_type=MESH)

    loads = [
        pltpu.make_async_copy(src, dst, in_sem.at[n])
        for n, (src, dst) in enumerate(
            (
                (img, tiles.at[48:96, 128:640]),
                (w0_in, w0_raw),
                (wm_in, wm_raw),
                (gains_in, norm_raw.at[0]),
                (shifts_in, norm_raw.at[1]),
                (cot, cot_raw),
            )
        )
    ]
    for load in loads:
        load.start()
    partners = [(hops((dy, dx, 0)), plane_peer((dy, dx, dc))[1]) for dy, dx, dc in PLANE_OFFSETS]
    partners += [(hops((0, 0, dz)), depth_peer(dz)) for dz in DEPTH_OFFSETS]
    partners.sort(key=lambda partner: -partner[0])
    for distance, where in partners:
        if distance >= 3:
            greet(where)
    for dr, dc in around:
        greet(near(dr, dc))
    for distance, where in partners:
        if distance < 3:
            greet(where)


    loads[0].wait()
    pl.semaphore_wait(barrier, len(around) + len(PLANE_OFFSETS) + len(DEPTH_OFFSETS))

    copies = []
    for n, (dr, dc) in enumerate(around):
        span = slice(128, 640) if dc == 0 else (slice(512, 640) if dc == 1 else slice(128, 256))
        lanes = slice(128, 640) if dc == 0 else (slice(0, 128) if dc == 1 else slice(640, 768))
        first = 48 * (1 - dr)
        copies.append(
            pltpu.make_async_remote_copy(
                src_ref=tiles.at[48:96, span],
                dst_ref=tiles.at[first : first + 48, lanes],
                send_sem=img_send.at[n],
                recv_sem=img_recv.at[n],
                device_id=near(dr, dc),
                device_id_type=MESH,
            )
        )
    for copy in copies:
        copy.start()

    def steps(v, edges):
        return sum(jnp.where(v >= e, 1, 0) for e in edges)

    src = lax.broadcasted_iota(jnp.int32, (512, 256), 0)
    dst = lax.broadcasted_iota(jnp.int32, (1, 256), 1)
    dst_q, dst_b = dst // 8, dst % 8
    dst_a = steps(dst_q, range(3, 21, 3))
    dst_c = dst_q - 3 * dst_a
    place = jnp.where((dst_b < 7) & (dst_q < 21), CH * dst_b + STEM_ROWS * dst_c + dst_a, -1)
    choose[...] = jnp.where(src == place, 1.0, 0.0).astype(BF16)
    diff = lax.broadcasted_iota(jnp.int32, (768, 384), 0) - 2 * lax.broadcasted_iota(
        jnp.int32, (768, 384), 1
    )
    sel[0] = jnp.where(diff == 124, 1.0, 0.0).astype(BF16)
    sel[1] = jnp.where(diff == 125, 1.0, 0.0).astype(BF16)

    m = lax.broadcasted_iota(jnp.int32, (64, 144), 0)
    n = lax.broadcasted_iota(jnp.int32, (64, 144), 1)
    m_c = steps(m, (21, 42, 63))
    m_r = m - 21 * m_c
    n_t = steps(n, (48, 96))
    n_in = n - 48 * n_t
    n_c = steps(n_in, (16, 32))
    n_r = 16 * n_t + n_in - 16 * n_c
    pick = jnp.where((m_c == n_c) & (n_r == m_r + 13), 1.0, 0.0).astype(BF16)

    w0_flat[...] = jnp.zeros(w0_flat.shape, F32)
    for load in loads[1:]:
        load.wait()

    for k in range(21):
        w0_flat[8 * k : 8 * k + 7, 0:CH] = w0_raw[k].astype(F32)
    w0 = dot_nt(w0_flat[...].T[0:CH, :].astype(BF16), choose[...])
    for i in range(ROWS):
        wbig[CH * i : CH * (i + 1), :] = (pltpu.roll(w0, 2 * i, 1) if i else w0).astype(BF16)
    w0_flat[0:3, 0:CH] = norm_raw[0]
    w0_flat[8:11, 0:CH] = norm_raw[1]
    columns = w0_flat[0:16, :].T
    gain = [columns[0:CH, k : k + 1] for k in range(3)]
    shift = [columns[0:CH, 8 + k : 9 + k] for k in range(3)]

    for copy in copies:
        copy.wait()

    def scale_tile(rows, lanes, factor):
        tiles[rows, lanes] = (tiles[rows, lanes].astype(F32) * factor).astype(BF16)

    scale_tile(slice(0, 48), slice(0, 768), not_top)
    scale_tile(slice(96, 144), slice(0, 768), not_bottom)
    scale_tile(slice(0, 144), slice(0, 128), not_left)
    scale_tile(slice(0, 144), slice(640, 768), not_right)

    image_rows = dot(pick, tiles[...]).astype(BF16)
    planes = [dot(image_rows, sel[0]), dot(image_rows, sel[1])]
    for b in range(7):
        shift_by = (b - 3) // 2 + 2
        plane = planes[(b - 3) % 2]
        moved = pltpu.roll(plane, 384 - shift_by, 1) if shift_by else plane
        patches[CH * b : CH * (b + 1), :] = moved[:, 0:COLS].astype(BF16)
    patches[448:512, :] = jnp.zeros((64, COLS), BF16)

    lane128 = lax.broadcasted_iota(jnp.int32, (CH, 128), 1)
    lane256 = lax.broadcasted_iota(jnp.int32, (CH, COLS), 1)
    lane1 = lax.broadcasted_iota(jnp.int32, (1, 128), 1)

    def fold(v):
        return v[:, 0:128] + v[:, 128:256]

    def to_row(first, second):
        both = jnp.where(lane128 == 0, first, jnp.where(lane128 == 1, second, 0.0)).T
        return jnp.concatenate([both[0:1, :], both[1:2, :]], axis=1)

    def to_columns(row_value):
        turned = jnp.broadcast_to(row_value, (8, 128)).T
        return turned[0:CH, 0:1], turned[CH : 2 * CH, 0:1]

    def drain(buf, count, sem):
        part = buf.at[0:count]
        pltpu.make_async_copy(part, part, sem).wait()

    def send(src, dst, send_sem, recv_sem, where):
        pltpu.make_async_remote_copy(
            src_ref=src,
            dst_ref=dst,
            send_sem=send_sem,
            recv_sem=recv_sem,
            device_id=where,
            device_id_type=MESH,
        ).start()

    def exchange(index, value, combine, before, within, meanwhile):
        if index == 0:
            return first_exchange(value, combine, before, within, meanwhile)
        buf, sems = ar_a.at[index], (ar_send.at[index, 0], ar_recv.at[index, 0])
        buf[pl.ds(core, 1)] = value[None]
        send(buf.at[core], buf.at[core], *sems, other_core)
        before()
        drain(buf, 1, sems[1])
        value = combine(buf[...], float(LOCAL))
        drain(buf, 1, sems[0])
        buf, sems = ar_b.at[index], (ar_send.at[index, 1], ar_recv.at[index, 1])
        buf[pl.ds(chip_rank, 1)] = value[None]
        for place, offset in enumerate(CHIP_OFFSETS):
            if hops(offset) == 3 and hops(CHIP_OFFSETS[place - 1]) == 4:
                within()
            send(buf.at[chip_rank], buf.at[chip_rank], *sems, chip_peer(offset))
        meanwhile()
        drain(buf, CHIPS - 1, sems[1])
        drain(buf, CHIPS - 1, sems[0])
        return combine(buf[...], float(LOCAL * 2))

    def first_exchange(value, combine, before, within, meanwhile):
        sems = (ar_send.at[0, 0], ar_recv.at[0, 0])
        first_a[pl.ds(plane_rank, 1)] = value[None]
        for offset in PLANE_OFFSETS:
            send(first_a.at[plane_rank], first_a.at[plane_rank], *sems, plane_peer(offset)[1])
        before()
        within()
        meanwhile()
        drain(first_a, PLANE - 1, sems[1])
        drain(first_a, PLANE - 1, sems[0])
        value = combine(first_a[...], float(LOCAL))
        sems = (ar_send.at[0, 1], ar_recv.at[0, 1])
        first_b[pl.ds(chip_z, 1)] = value[None]
        for dz in DEPTH_OFFSETS:
            where = depth_peer(dz)
            send(first_b.at[chip_z], first_b.at[chip_z], *sems, where)
        drain(first_b, DEPTH - 1, sems[1])
        drain(first_b, DEPTH - 1, sems[0])
        return combine(first_b[...], float(LOCAL * PLANE))

    def total_of(got):
        if got.shape[0] == CHIPS:
            got = jnp.sum(got.reshape(8, 16, 1, 128), axis=0)
        return jnp.sum(got, axis=0)

    def combine_moments(got, count):
        total = total_of(got)
        mean = total * (1.0 / got.shape[0])
        off = got - mean[None]
        spread = total_of(off * off) * count
        return jnp.where(lane1 < CH, mean, total + pltpu.roll(spread, CH, 1))

    def combine_sums(got, count):
        return total_of(got)

    def pack_halo(index, ref):
        for side, lane in ((0, 0), (1, COLS - 1)):
            pack = jnp.zeros((CH, 128), F32)
            for i in range(ROWS):
                pack = jnp.where(lane128 == i, ref[i, :, lane : lane + 1], pack)
            pack = jnp.concatenate([pack, jnp.zeros((128 - CH, 128), F32)], axis=0)
            colsend[index, side] = pack.T[0:ROWS, :]

    def send_halo(index, ref):
        started = []
        for n, (dr, dc) in enumerate(around):
            if dc == 0:
                src = ref.at[ROWS - 1 if dr == 1 else 0]
                dst = rowhalo.at[index, 0 if dr == 1 else 1]
            else:
                src = colsend.at[index, 1 if dc == 1 else 0]
                dst = colrecv.at[index, (0 if dc == 1 else 3) + 1 - dr]
            copy = pltpu.make_async_remote_copy(
                src_ref=src,
                dst_ref=dst,
                send_sem=halo_send.at[index, n],
                recv_sem=halo_recv.at[index, n],
                device_id=near(dr, dc),
                device_id_type=MESH,
            )
            copy.start()
            started.append(copy)
        return started

    def build(dst, center, top, bottom, sides):
        for r in range(ROWS + 2):
            value = top if r == 0 else (bottom if r == ROWS + 1 else center(r - 1))
            lane = ROWS - 1 if r == 0 else (2 * ROWS if r == ROWS + 1 else ROWS + r - 1)
            before = jnp.where(lane256 == 0, sides[:, lane : lane + 1], pltpu.roll(value, 1, 1))
            lane += 3 * ROWS
            after = jnp.where(
                lane256 == COLS - 1, sides[:, lane : lane + 1], pltpu.roll(value, COLS - 1, 1)
            )
            base = 3 * CH * r
            dst[base : base + CH, :] = before.astype(BF16)
            dst[base + CH : base + 2 * CH, :] = value.astype(BF16)
            dst[base + 2 * CH : base + 3 * CH, :] = after.astype(BF16)

    lane48 = lax.broadcasted_iota(jnp.int32, (1, 6 * ROWS), 1)
    edge = jnp.where(lane48 < 3 * ROWS, not_left, not_right)
    in_side = jnp.where(lane48 < 3 * ROWS, lane48, lane48 - 3 * ROWS)
    edge = edge * jnp.where(in_side < ROWS, not_top, jnp.where(in_side < 2 * ROWS, 1.0, not_bottom))

    def build_with_halo(dst, center, apply_halo, index):
        top = apply_halo("row", 0) * not_top
        bottom = apply_halo("row", 1) * not_bottom
        build(dst, center, top, bottom, apply_halo("col", None) * edge)

    def conv(weight, src, out, after=None):
        for i in range(ROWS):
            value = dot(weight, src[3 * CH * i : 3 * CH * i + TAPS, :])
            out[i] = value if after is None else after(i, value)

    def moments(index, *hidden):
        ref = pre.at[index]
        total = jnp.zeros((CH, 128), F32)
        for i in range(ROWS):
            total = total + fold(ref[i])
        mean = jnp.sum(total, axis=1, keepdims=True) * (1.0 / LOCAL)
        total = jnp.zeros((CH, 128), F32)
        for i in range(ROWS):
            off = ref[i] - mean
            total = total + fold(off * off)
        local = to_row(mean, jnp.sum(total, axis=1, keepdims=True))
        mean, squares = to_columns(exchange(index, local, combine_moments, *hidden))
        return mean, lax.rsqrt(squares * (1.0 / PIXELS) + EPS)

    def halo_block(index, kind, place):
        if kind == "row":
            return rowhalo[index, place]
        return colrecv[index].reshape(6 * ROWS, 128).T[0:CH, :]

    mean, inv = [None] * 3, [None] * 3

    def forward_norm(index, meanwhile):
        halo, ref = [], pre.at[index]
        mean[index], inv[index] = moments(
            index,
            lambda: pack_halo(index, ref),
            lambda: halo.extend(send_halo(index, ref)),
            meanwhile,
        )
        for copy in halo:
            copy.wait()

    def forward_rows(index, i):
        normed_white = (pre[index, i] - mean[index]) * inv[index]
        white[index, i] = normed_white
        normed = gain[index] * normed_white + shift[index]
        sig = jax.nn.sigmoid(normed)
        slope[index, i] = sig * (1.0 + normed * (1.0 - sig))
        return normed * sig

    def forward_build(index, dst):
        def outside(kind, place):
            block = halo_block(index, kind, place)
            normed = gain[index] * ((block - mean[index]) * inv[index]) + shift[index]
            return normed * jax.nn.sigmoid(normed)

        build_with_halo(dst, lambda i: forward_rows(index, i), outside, index)

    def taps_of(layer):
        return [wm_raw[9 * layer + t].astype(F32) for t in range(9)]

    def lay_taps(parts, target):
        for t in range(0, 9, 2):
            part = parts[t : t + 2]
            value = jnp.concatenate(part, axis=1) if len(part) == 2 else part[0]
            target[:, CH * t : CH * (t + len(part))] = value.astype(BF16)

    def lay_weights():
        for layer in range(2):
            lay_taps(taps_of(layer), wm.at[layer])

    def lay_turned():
        gsend[...] = jnp.zeros(gsend.shape, F32)
        for layer in range(2):
            parts = taps_of(layer)
            lay_taps([parts[8 - t].T for t in range(9)], wt.at[layer])

    def spread_cotangent():
        cot_flat[...] = cot_raw[...].astype(F32)
        for i in range(ROWS):
            cot_rows[i] = cot_flat[:, i, :]

    stem = dot(wbig[...], patches[...])
    for i in range(ROWS):
        pre[0, i] = stem[CH * i : CH * (i + 1), :]
    forward_norm(0, lay_weights)
    forward_build(0, x0)
    conv(wm[0], x0, pre.at[1])
    forward_norm(1, spread_cotangent)
    forward_build(1, x1)
    conv(wm[1], x1, pre.at[2])
    forward_norm(2, lay_turned)
    for i in range(ROWS):
        act_rows[i] = forward_rows(2, i)
        up[2, i] = cot_rows[i] * slope[2, i]

    def norm_sums(index, *hidden):
        shift_total = jnp.zeros((CH, 128), F32)
        gain_total = jnp.zeros((CH, 128), F32)
        for i in range(ROWS):
            shift_total = shift_total + fold(up[index, i])
            gain_total = gain_total + fold(up[index, i] * white[index, i])
        local = to_row(
            jnp.sum(shift_total, axis=1, keepdims=True), jnp.sum(gain_total, axis=1, keepdims=True)
        )
        sums = exchange(3 + index, local, combine_sums, *hidden)
        shifts_out[index : index + 1, :] = sums[:, 0:CH]
        gains_out[index : index + 1, :] = sums[:, CH : 2 * CH]
        shift_sum, gain_sum = to_columns(sums)
        return shift_sum * (1.0 / PIXELS), gain_sum * (1.0 / PIXELS)

    def down(index, sums, up_value, whitened):
        return (gain[index] * inv[index]) * (up_value - sums[0] - whitened * sums[1])

    def backward_norm(index, halo_index, meanwhile):
        halo, ref = [], up.at[index]
        sums = norm_sums(
            index,
            lambda: pack_halo(halo_index, ref),
            lambda: halo.extend(send_halo(halo_index, ref)),
            meanwhile,
        )

        def center(i):
            return down(index, sums, up[index, i], white[index, i])

        def outside(kind, place):
            whitened = (halo_block(index, kind, place) - mean[index]) * inv[index]
            return down(index, sums, halo_block(halo_index, kind, place), whitened)

        for copy in halo:
            copy.wait()
        build_with_halo(dmap, center, outside, index)

    def kernel_grad(src):
        total = jnp.zeros((CH, TAPS), F32)
        for i in range(ROWS):
            base = 3 * CH * (i + 1) + CH
            total = total + dot_nt(dmap[base : base + CH, :], src[3 * CH * i : 3 * CH * i + TAPS, :])
        return total

    def put(buf, value):
        for k in range(PLANE):
            buf[k, :, 0 : value.shape[1]] = value[2 * k : 2 * k + 2, :]

    def scatter(n, mine, got):
        got[pl.ds(plane_rank, 1)] = mine[pl.ds(plane_rank, 1)]
        for offset in PLANE_OFFSETS:
            rank, where = plane_peer(offset)
            send(mine.at[rank], got.at[plane_rank], fin_send.at[n, 0], fin_recv.at[n, 0], where)

    def along_depth(n, got, depth):
        drain(got, PLANE - 1, fin_recv.at[n, 0])
        depth[pl.ds(chip_z, 1)] = jnp.sum(got[...], axis=0)[None]
        for dz in DEPTH_OFFSETS:
            where = depth_peer(dz)
            send(depth.at[chip_z], depth.at[chip_z], fin_send.at[n, 1], fin_recv.at[n, 1], where)

    def spread(n, depth, full):
        drain(depth, DEPTH - 1, fin_recv.at[n, 1])
        full[pl.ds(plane_rank, 1)] = jnp.sum(depth[...], axis=0)[None]
        for offset in PLANE_OFFSETS:
            where = plane_peer(offset)[1]
            send(full.at[plane_rank], full.at[plane_rank], fin_send.at[n, 2], fin_recv.at[n, 2], where)

    def collect(n, full, lanes):
        drain(full, PLANE - 1, fin_recv.at[n, 2])
        for k in range(PLANE):
            rows_full[2 * k : 2 * k + 2, 0:lanes] = full[k]

    leaving = []

    def leave(src, dst):
        copy = pltpu.make_async_copy(src, dst, out_sem.at[len(leaving)])
        copy.start()
        leaving.append(copy)

    def finish_mid(layer):
        collect(layer, gfull.at[layer], 640)
        for t in range(9):
            mid_out[9 * layer + t] = rows_full[:, CH * t : CH * (t + 1)]
        span = pl.ds(9 * layer, 9)
        leave(mid_out.at[span], mid_hbm.at[span])

    def grad_stage_1(layer, src):
        put(gsend.at[layer], kernel_grad(src))
        scatter(layer, gsend.at[layer], grecv.at[layer])

    def turn_activation():
        for i in range(ROWS):
            cot_flat[:, i, :] = act_rows[i]
        act_out[...] = cot_flat[...].astype(BF16)
        leave(act_out, act_hbm)

    backward_norm(2, 3, turn_activation)
    conv(wt[1], dmap, up.at[1], lambda i, value: value * slope[1, i])
    backward_norm(1, 4, lambda: grad_stage_1(1, x1))
    conv(wt[0], dmap, up.at[0], lambda i, value: value * slope[0, i])

    def last_shadow():
        along_depth(1, grecv.at[1], gdepth.at[1])
        grad_stage_1(0, x0)

    def nothing():
        pass

    sums = norm_sums(0, nothing, nothing, last_shadow)
    leave(gains_out, gains_hbm)
    leave(shifts_out, shifts_hbm)
    for i in range(ROWS):
        dstem[CH * i : CH * (i + 1), :] = down(0, sums, up[0, i], white[0, i]).astype(BF16)
    banded = dot_nt(dstem[...], patches[...])
    total = banded[0:CH, :]
    for i in range(1, ROWS):
        total = total + pltpu.roll(banded[CH * i : CH * (i + 1), :], 512 - 2 * i, 1)
    high = total.astype(BF16)
    rest = total - high.astype(F32)
    mid = rest.astype(BF16)
    low = (rest - mid.astype(F32)).astype(BF16)
    put(ssend, dot(high, choose[...]) + dot(mid, choose[...]) + dot(low, choose[...]))
    scatter(2, ssend, srecv)
    along_depth(0, grecv.at[0], gdepth.at[0])
    spread(1, gdepth.at[1], gfull.at[1])
    along_depth(2, srecv, sdepth)
    spread(0, gdepth.at[0], gfull.at[0])
    finish_mid(1)
    spread(2, sdepth, sfull)
    finish_mid(0)
    collect(2, sfull, 256)
    turned = rows_full[:, 0:256].T
    stem_out[...] = turned[0:168, :].reshape(STEM_ROWS, 8, CH)[:, 0:7, :]
    leave(stem_out, stem_hbm)
    for n, (a, b, c) in enumerate(
        ((gsend.at[0], gdepth.at[0], gfull.at[0]), (gsend.at[1], gdepth.at[1], gfull.at[1]), (ssend, sdepth, sfull))
    ):
        drain(a, PLANE - 1, fin_send.at[n, 0])
        drain(b, DEPTH - 1, fin_send.at[n, 1])
        drain(c, PLANE - 1, fin_send.at[n, 2])
    for copy in leaving:
        copy.wait()


def write_out(*refs):
    ins, outs, held, sems = refs[0:5], refs[5:10], refs[10:15], refs[15]
    arriving = [pltpu.make_async_copy(a, b, sems.at[0, n]) for n, (a, b) in enumerate(zip(ins, held))]
    leaving = [pltpu.make_async_copy(a, b, sems.at[1, n]) for n, (a, b) in enumerate(zip(held, outs))]
    for copy in arriving:
        copy.start()
    for first, second in zip(arriving, leaving):
        first.wait()
        second.start()
    for copy in leaving:
        copy.wait()


def shards(slide_band, cotangent, stem_weight, mid_weight, norm_gains, norm_shifts):
    img = slide_band.reshape(48, 512)
    w0 = stem_weight.transpose(1, 3, 2, 0).reshape(STEM_ROWS, 7, CH)
    wm = mid_weight.transpose(0, 2, 3, 1, 4).reshape(18, CH, CH)
    hbm = pl.BlockSpec(memory_space=pltpu.HBM)
    dma = pltpu.SemaphoreType.DMA
    shapes = (
        jax.ShapeDtypeStruct((CH, ROWS, COLS), BF16),
        jax.ShapeDtypeStruct((STEM_ROWS, 7, CH), F32),
        jax.ShapeDtypeStruct((18, CH, CH), F32),
        jax.ShapeDtypeStruct((3, CH), F32),
        jax.ShapeDtypeStruct((3, CH), F32),
    )
    results = pl.pallas_call(
        kernel,
        out_shape=shapes,
        in_specs=[hbm] * 6,
        out_specs=(hbm,) * 5,
        scratch_shapes=[
            pltpu.VMEM((CH, ROWS, COLS), BF16),
            pltpu.VMEM((STEM_ROWS, 7, CH), F32),
            pltpu.VMEM((18, CH, CH), F32),
            pltpu.VMEM((3, CH), F32),
            pltpu.VMEM((3, CH), F32),
            pltpu.VMEM((CH, ROWS, COLS), BF16),
            pltpu.VMEM((STEM_ROWS, 7, CH), BF16),
            pltpu.VMEM((18, CH, CH), BF16),
            pltpu.VMEM((2, 3, CH), F32),
            pltpu.VMEM((256, 128), F32),
            pltpu.VMEM((2, CH, TAPS), BF16),
            pltpu.VMEM((2, CH, TAPS), BF16),
            pltpu.VMEM((CH, ROWS, COLS), F32),
            pltpu.VMEM((ROWS, CH, COLS), F32),
            pltpu.VMEM((ROWS, CH, COLS), F32),
            pltpu.VMEM((512, 256), BF16),
            pltpu.VMEM((144, 768), BF16),
            pltpu.VMEM((2, 768, 384), BF16),
            pltpu.VMEM((512, COLS), BF16),
            pltpu.VMEM((512, 512), BF16),
            pltpu.VMEM((3 * CH * (ROWS + 2), COLS), BF16),
            pltpu.VMEM((3 * CH * (ROWS + 2), COLS), BF16),
            pltpu.VMEM((3 * CH * (ROWS + 2), COLS), BF16),
            pltpu.VMEM((512, COLS), BF16),
            pltpu.VMEM((3, ROWS, CH, COLS), F32),
            pltpu.VMEM((3, ROWS, CH, COLS), F32),
            pltpu.VMEM((3, ROWS, CH, COLS), F32),
            pltpu.VMEM((3, ROWS, CH, COLS), F32),
            pltpu.VMEM((5, 2, CH, COLS), F32),
            pltpu.VMEM((5, 2, ROWS, 128), F32),
            pltpu.VMEM((5, 6, ROWS, 128), F32),
            pltpu.VMEM((PLANE, 1, 128), F32),
            pltpu.VMEM((DEPTH, 1, 128), F32),
            pltpu.VMEM((6, 2, 1, 128), F32),
            pltpu.VMEM((6, CHIPS, 1, 128), F32),
            pltpu.VMEM((2, PLANE, 2, 640), F32),
            pltpu.VMEM((2, PLANE, 2, 640), F32),
            pltpu.VMEM((2, DEPTH, 2, 640), F32),
            pltpu.VMEM((2, PLANE, 2, 640), F32),
            pltpu.VMEM((PLANE, 2, 256), F32),
            pltpu.VMEM((PLANE, 2, 256), F32),
            pltpu.VMEM((DEPTH, 2, 256), F32),
            pltpu.VMEM((PLANE, 2, 256), F32),
            pltpu.VMEM((CH, 640), F32),
            dma((6,)), dma((6,)),
            dma((8,)), dma((8,)), dma((5, 8)), dma((5, 8)),
            dma((6, 2)), dma((6, 2)), dma((3, 3)), dma((3, 3)),
        ],
        compiler_params=pltpu.CompilerParams(
            collective_id=0, has_side_effects=True, vmem_limit_bytes=VMEM_BYTES
        ),
    )(img, cotangent, w0, wm, norm_gains, norm_shifts)
    act, stem, mid, gains, shifts = pl.pallas_call(
        write_out,
        out_shape=shapes,
        in_specs=[hbm] * 5,
        out_specs=(hbm,) * 5,
        scratch_shapes=[pltpu.VMEM(a.shape, a.dtype) for a in shapes] + [dma((2, 5))],
        compiler_params=pltpu.CompilerParams(vmem_limit_bytes=VMEM_BYTES),
    )(*results)
    return (
        act,
        stem.reshape(7, 3, 7, CH).transpose(3, 0, 2, 1),
        mid.reshape(2, 3, 3, CH, CH).transpose(0, 3, 1, 2, 4),
        gains,
        shifts,
    )


def solution(mesh):
    return jax.shard_map(
        shards,
        mesh=mesh,
        in_specs=(P(None, "row", "col"), P(None, "row", "col"), P(), P(), P(), P()),
        out_specs=(P(None, "row", "col"), P(), P(), P(), P()),
        check_vma=False,
    )
```

profile of v0, /device:TPU:1, one launch (start us, length us, event | category | flops | bytes accessed | tf_op | source)
XLA Modules:
  0.0 91.3 jit_solution(2770927126261886811)
XLA Ops:
  0.6 88.4 %shard_map.101 = (bf16[64,8,256]{2,1,0:T(8,128)(2,1)}, f32[21,7,64]{2,1,0:T(8,128)}, f32[18,64,64]{2,1,0:T(8,128)}, f32[3,64]{1,0:T(4,128)}, f32[3,64]{1,0:T(4,128)}) custom-call(bf16[48,512]{1,0:T(8,128)(2,1)} %bitcast.14, bf16[64,8,256]{2,1,0:T(8,128)(2,1)} %cot.1, bf16[21,7,64]{2,1,0:T(8,128)(2,1)} %bitcast.15, bf16[18,64,64]{2,1,0:T(8,128)(2,1)} %bitcast.13, ...), custom_call_target="tpu_custom_call" | custom-call | tf_op jit(solution)/shard_map/pallas_call | solution.py:608
  89.1 2.1 %shard_map.102 = (bf16[64,8,256]{2,1,0:T(8,128)(2,1)}, f32[21,7,64]{2,1,0:T(8,128)}, f32[18,64,64]{2,1,0:T(8,128)}, f32[3,64]{1,0:T(4,128)}, f32[3,64]{1,0:T(4,128)}) custom-call(bf16[64,8,256]{2,1,0:T(8,128)(2,1)} %get-tuple-element.15.refs_0_, f32[21,7,64]{2,1,0:T(8,128)} %get-tuple-element.16.refs_1_, f32[18,64,64]{2,1,0:T(8,128)} %get-tuple-element.17.refs_2_, ...), custom_call_target="tpu_custom_call" | custom-call | tf_op jit(solution)/shard_map/pallas_call | solution.py:666
where the time goes:
time: 91.4 us; the launch traced here: 91.3 us
  Pallas kernels  90.5 us (99%)
    pallas_call x1, Pallas kernels, shards(): pl.pallas_call(kernel, out_shape=shapes, in_specs=[hbm] * 6, out_specs=(h...  88.4 us
    pallas_call x1, Pallas kernels, shards(): pl.pallas_call(write_out, out_shape=shapes, in_specs=[hbm] * 5, out_specs...  2.09 us

commit v1 on v0

--- a/solution.py
+++ b/solution.py
@@ -345,13 +345,13 @@
     def conv(weight, src, out, after=None):
         for i in range(ROWS):
             value = dot(weight, src[3 * CH * i : 3 * CH * i + TAPS, :])
+            if after is None:
+                total = fold(value) if i == 0 else total + fold(value)
             out[i] = value if after is None else after(i, value)
-
-    def moments(index, *hidden):
+        return total if after is None else None
+
+    def moments(index, total, *hidden):
         ref = pre.at[index]
-        total = jnp.zeros((CH, 128), F32)
-        for i in range(ROWS):
-            total = total + fold(ref[i])
         mean = jnp.sum(total, axis=1, keepdims=True) * (1.0 / LOCAL)
         total = jnp.zeros((CH, 128), F32)
         for i in range(ROWS):
@@ -368,10 +368,11 @@
 
     mean, inv = [None] * 3, [None] * 3
 
-    def forward_norm(index, meanwhile):
+    def forward_norm(index, total, meanwhile):
         halo, ref = [], pre.at[index]
         mean[index], inv[index] = moments(
             index,
+            total,
             lambda: pack_halo(index, ref),
             lambda: halo.extend(send_halo(index, ref)),
             meanwhile,
@@ -422,13 +423,14 @@
     stem = dot(wbig[...], patches[...])
     for i in range(ROWS):
         pre[0, i] = stem[CH * i : CH * (i + 1), :]
-    forward_norm(0, lay_weights)
+    total = sum(fold(stem[CH * i : CH * (i + 1), :]) for i in range(ROWS))
+    forward_norm(0, total, lay_weights)
     forward_build(0, x0)
-    conv(wm[0], x0, pre.at[1])
-    forward_norm(1, spread_cotangent)
+    total = conv(wm[0], x0, pre.at[1])
+    forward_norm(1, total, spread_cotangent)
     forward_build(1, x1)
-    conv(wm[1], x1, pre.at[2])
-    forward_norm(2, lay_turned)
+    total = conv(wm[1], x1, pre.at[2])
+    forward_norm(2, total, lay_turned)
     for i in range(ROWS):
         act_rows[i] = forward_rows(2, i)
         up[2, i] = cot_rows[i] * slope[2, i]

time: 91.4 us -> 91.4 us (level)
  no operation moved by 1% of the time
where the time goes in v1:
time: 91.4 us; the launch traced here: 91.3 us
  Pallas kernels  90.5 us (99%)
    pallas_call x1, Pallas kernels, shards(): pl.pallas_call(kernel, out_shape=shapes, in_specs=[hbm] * 6, out_specs=(h...  88.4 us
    pallas_call x1, Pallas kernels, shards(): pl.pallas_call(write_out, out_shape=shapes, in_specs=[hbm] * 5, out_specs...  2.09 us

profile of v1, /device:TPU:1, one launch (start us, length us, event | category | flops | bytes accessed | tf_op | source)
XLA Modules:
  0.0 91.3 jit_solution(894026808766164476)
XLA Ops:
  0.6 88.4 %shard_map.101 = (bf16[64,8,256]{2,1,0:T(8,128)(2,1)}, f32[21,7,64]{2,1,0:T(8,128)}, f32[18,64,64]{2,1,0:T(8,128)}, f32[3,64]{1,0:T(4,128)}, f32[3,64]{1,0:T(4,128)}) custom-call(bf16[48,512]{1,0:T(8,128)(2,1)} %bitcast.14, bf16[64,8,256]{2,1,0:T(8,128)(2,1)} %cot.1, bf16[21,7,64]{2,1,0:T(8,128)(2,1)} %bitcast.15, bf16[18,64,64]{2,1,0:T(8,128)(2,1)} %bitcast.13, ...), custom_call_target="tpu_custom_call" | custom-call | tf_op jit(solution)/shard_map/pallas_call | solution.py:610
  89.0 2.1 %shard_map.102 = (bf16[64,8,256]{2,1,0:T(8,128)(2,1)}, f32[21,7,64]{2,1,0:T(8,128)}, f32[18,64,64]{2,1,0:T(8,128)}, f32[3,64]{1,0:T(4,128)}, f32[3,64]{1,0:T(4,128)}) custom-call(bf16[64,8,256]{2,1,0:T(8,128)(2,1)} %get-tuple-element.15.refs_0_, f32[21,7,64]{2,1,0:T(8,128)} %get-tuple-element.16.refs_1_, f32[18,64,64]{2,1,0:T(8,128)} %get-tuple-element.17.refs_2_, ...), custom_call_target="tpu_custom_call" | custom-call | tf_op jit(solution)/shard_map/pallas_call | solution.py:668
